TPU v7x, 512 devices: a whole 4x4x16 slice. The times are simulated.
512 devices in a mesh: dof: 16 (over y, z_hi), atom: 32 (over x, z_lo, core).
Axes of the slice: x: 4, y: 4, z: 16 (z_hi: 4, z_lo: 4; z = z_hi * 4 + z_lo), core: 2. Of those that a mesh axis runs over, the one named last changes fastest.
Arguments:
- received: bfloat16 [2, 64, 8192], P(None, None, 'dof'), may hold values from -6 to 6
- codes_now: bfloat16 [2, 64, 65536], P(None, 'dof', 'atom'), may hold values from -6 to 6
- ridge_tiles: bfloat16 [16, 32, 4, 2, 128, 128], P('dof', 'atom'), may hold values from -0.0625 to 0.0625
- coords: int32 [16, 32, 4, 2], P('dof', 'atom'), may hold values from 0 to 15, as said below
- tile_counts: int32 [16, 32], P('dof', 'atom'), may hold values from 1 to 4, as said below
- group_ids: int32 [512], P('atom'), may hold values from 0 to 7
- thresholds: float32 [8], replicated, may hold values from 0.1 to 1
- cotangent: bfloat16 [2, 64, 65536], P(None, 'dof', 'atom'), may hold values from -6 to 6
Outputs:
- codes_next: bfloat16 [2, 64, 65536], P(None, 'dof', 'atom')
- tile_grads: bfloat16 [16, 32, 4, 2, 128, 128], P('dof', 'atom')
- threshold_grads: float32 [8], replicated
Inputs may be any that keep to these rules, and one draw needn't show every extreme that they name: coords[p, q, l] = (row tile under 0 to 3, atom tile under 0 to 15) of device (p, q); row tiles follow the atom tiles along a ridge; a pair may repeat. Slots l >= tile_counts of a device are empty; some device has all 4 live.
All inputs are finite; a program needn't handle non-finite values.
Results may differ from a plain program's by a relative error of at most 0.03565.
The roundings to bfloat16 on the way count: a program that leaves them out, or rounds other values in their place, can miss the bound.
Values may be sent and summed in bfloat16 or wider, within the bound.
A program may use at most 192 MiB of HBM per device.

v0:
```python
import jax
import jax.numpy as jnp
from jax import lax
from jax.sharding import PartitionSpec as P


def shrink(field, theta_atom):
    magnitude = jnp.sqrt(field[0] * field[0] + field[1] * field[1] + 1e-06)
    factor = jnp.maximum(magnitude - theta_atom, 0.0) / jnp.maximum(magnitude, theta_atom)
    return field * factor


def ridge_apply(tiles_live, codes_block, col_index, rows_hot):
    halves, snapshots, columns = codes_block.shape
    tile_size = tiles_live.shape[-1]
    blocks = codes_block.reshape(halves, snapshots, columns // tile_size, tile_size)
    picked = jnp.take(blocks, col_index, axis=2)
    product = jnp.einsum("lcab,dslb->cdsla", tiles_live, picked, preferred_element_type=jnp.float32)
    stacked = jnp.stack([product[0, 0] - product[1, 1], product[0, 1] + product[1, 0]])
    placed = jnp.einsum("esla,lr->esra", stacked, rows_hot, precision=lax.Precision.HIGHEST)
    return placed.reshape(halves, snapshots, -1)


def ridge_adjoint(tiles_live, resid_block, row_index, cols_hot):
    halves, snapshots, rows_width = resid_block.shape
    tile_size = tiles_live.shape[-1]
    blocks = resid_block.reshape(halves, snapshots, rows_width // tile_size, tile_size)
    picked = jnp.take(blocks, row_index, axis=2)
    product = jnp.einsum("lcab,dsla->cdslb", tiles_live, picked, preferred_element_type=jnp.float32)
    stacked = jnp.stack([product[0, 0] + product[1, 1], product[0, 1] - product[1, 0]])
    placed = jnp.einsum("eslb,lk->eskb", stacked, cols_hot, precision=lax.Precision.HIGHEST)
    return placed.reshape(halves, snapshots, -1)


def ridge_grads(resid_block, grad_codes, grad_resid, codes_block, row_index, col_index, tile_size):
    halves, snapshots, rows_width = resid_block.shape
    atoms_width = codes_block.shape[2]

    def pick(array, width, index):
        return jnp.take(
            array.reshape(halves, snapshots, width // tile_size, tile_size), index, axis=2
        )

    left = jnp.einsum(
        "csla,dslb->cdlab",
        pick(resid_block, rows_width, row_index),
        pick(grad_codes, atoms_width, col_index),
        preferred_element_type=jnp.float32,
    )
    right = jnp.einsum(
        "csla,dslb->cdlab",
        pick(grad_resid, rows_width, row_index),
        pick(codes_block, atoms_width, col_index),
        preferred_element_type=jnp.float32,
    )
    grad_real = left[0, 0] + left[1, 1] - right[0, 0] - right[1, 1]
    grad_imag = left[1, 0] - left[0, 1] + right[0, 1] - right[1, 0]
    return jnp.stack([grad_real, grad_imag], axis=1)


def threshold_step(base, correlation, groups, thresholds, cot_part):
    field = base.astype(jnp.float32) + correlation
    onehot = (groups[:, None] == jnp.arange(thresholds.shape[0])[None, :]).astype(jnp.float32)
    theta_atom = jnp.dot(onehot, thresholds, precision=lax.Precision.HIGHEST)
    shrunk, pull = jax.vjp(shrink, field, theta_atom)
    grad_field, grad_theta = pull(cot_part.astype(jnp.float32))
    theta_part = jnp.dot(grad_theta, onehot, precision=lax.Precision.HIGHEST)
    return (shrunk.astype(jnp.bfloat16), grad_field.astype(jnp.bfloat16), theta_part)


def local(received, codes_now, ridge_tiles, coords, tile_counts, group_ids, thresholds, cotangent):
    tile_set = ridge_tiles[0, 0]
    coord_set = coords[0, 0]
    slot_count = tile_set.shape[0]
    tile_size = tile_set.shape[-1]
    live = (jnp.arange(slot_count) < tile_counts[0, 0]).astype(jnp.float32)
    tiles_live = tile_set * live.astype(jnp.bfloat16)[:, None, None, None]
    rows_dev = received.shape[2]
    atoms_dev = codes_now.shape[2]
    rows_hot = (coord_set[:, 0][:, None] == jnp.arange(rows_dev // tile_size)[None, :]).astype(
        jnp.float32
    )
    cols_hot = (coord_set[:, 1][:, None] == jnp.arange(atoms_dev // tile_size)[None, :]).astype(
        jnp.float32
    )
    codes_all = lax.all_gather(codes_now, "dof", axis=1, tiled=True)
    fit_part = ridge_apply(tiles_live, codes_all, coord_set[:, 1], rows_hot)
    fitted = lax.psum(fit_part, "atom")
    residual = (received.astype(jnp.float32) - fitted).astype(jnp.bfloat16)
    group_atoms = jnp.repeat(group_ids, tile_size)
    corr_part = ridge_adjoint(tiles_live, residual, coord_set[:, 0], cols_hot)
    correlation = lax.psum_scatter(corr_part, "dof", scatter_dimension=1, tiled=True)
    codes_next, grad_share, theta_part = threshold_step(
        codes_now, correlation, group_atoms, thresholds, cotangent
    )
    grad_codes = lax.all_gather(grad_share, "dof", axis=1, tiled=True)
    threshold_grads = lax.psum(theta_part, ("dof", "atom"))
    back_part = ridge_apply(tiles_live, grad_codes, coord_set[:, 1], rows_hot)
    grad_resid = lax.psum(back_part.astype(jnp.bfloat16), "atom")
    grads = ridge_grads(
        residual, grad_codes, grad_resid, codes_all, coord_set[:, 0], coord_set[:, 1], tile_size
    )
    tile_grads = (grads * live[:, None, None, None]).astype(jnp.bfloat16)[None, None]
    return (codes_next, tile_grads, threshold_grads)


def solution(mesh):
    placed = (
        P(None, None, "dof"),
        P(None, "dof", "atom"),
        P("dof", "atom", None, None, None, None),
        P("dof", "atom", None, None),
        P("dof", "atom"),
        P("atom"),
        P(),
        P(None, "dof", "atom"),
    )
    return jax.shard_map(
        local,
        mesh=mesh,
        in_specs=placed,
        out_specs=(P(None, "dof", "atom"), P("dof", "atom", None, None, None, None), P()),
        check_vma=False,
    )
```

profile of v0, /device:TPU:1, one launch (start us, length us, event | category | flops | bytes accessed | tf_op | source)
XLA Modules:
  0.0 998.3 jit_solution(4657293103847395904)
XLA Ops:
  7.2 0.6 copy-done.5
  8.6 0.8 copy.77
  9.4 58.0 %all_gather.6 = bf16[2,64,2048]{2,0,1:T(2,128)(2,1)S(1)} all-gather(bf16[2,4,2048]{2,0,1:T(2,128)(2,1)S(1)} %copy.77), channel_id=1, replica_groups=mesh['dof'=16,'atom'=32] {'dof'}, dimensions={1}, use_global_device_ids=true | all-gather | bytes 557056 | tf_op jit(solution)/shard_map/all_gather | solution.py:86
  67.4 0.3 reshape.437
  68.0 0.6 gather_fusion
  68.5 0.4 copy-done.1
  69.3 0.5 convolution_bitcast_fusion.6
  69.8 0.8 reshape.376
  70.7 284.7 %all-reduce.7.cloned.1.call-done = f32[2,64,512]{2,1,0:T(8,128)} async-done(((f32[2,64,512]{2,1,0:T(8,128)}), f32[2,64,512]{2,1,0:T(8,128)}) %all-reduce.7.cloned.1.call-update) | async-done | bytes 262160 | tf_op jit(solution)/shard_map/psum | solution.py:88
  355.4 1.0 copy_bitcast_fusion
  356.4 0.6 gather_fusion.1
  357.3 0.8 convolution_bitcast_fusion.2
  358.1 1.2 reshape.378
  359.4 1.3 dynamic-slice
  361.4 0.6 copy-done.6
  362.0 0.7 fusion.1
  362.7 198.7 %all-reduce.11.cloned.1.call-done = f32[2,64,2048]{2,1,0:T(8,128)} async-done(((f32[2,64,2048]{2,1,0:T(8,128)}), f32[2,64,2048]{2,1,0:T(8,128)}) %all-reduce.11.cloned.1.call-update) | async-done | bytes 1048592
  561.4 1.0 fusion.36
  562.5 0.6 convolution_bitcast_fusion.7
  563.1 0.7 fusion.37
  563.8 47.3 %all_gather.7 = bf16[2,64,2048]{2,0,1:T(2,128)(2,1)S(1)} all-gather(bf16[2,4,2048]{2,0,1:T(2,128)(2,1)S(1)} %copy.87), channel_id=1, replica_groups=mesh['dof'=16,'atom'=32] {'dof'}, dimensions={1}, use_global_device_ids=true | all-gather | bytes 557056 | tf_op jit(solution)/shard_map/all_gather | solution.py:96
  611.1 0.3 reshape.438
  611.6 0.6 gather_fusion.2
  612.2 0.3 convolution_bitcast_fusion.3
  612.6 119.2 %psum.23 = f32[8]{0:T(128)} all-reduce(f32[8]{0:T(128)S(1)} %convolution_bitcast_fusion.7), channel_id=1, replica_groups=mesh['dof'=16,'atom'=32] {'dof','atom'}, use_global_device_ids=true, to_apply=%region_6.9 | all-reduce | flops 8 | bytes 64 | tf_op jit(solution)/shard_map/psum | solution.py:97
  731.8 1.2 fusion
  733.0 0.4 convolution_bitcast_fusion.1
  733.4 255.4 %all-reduce.9.cloned.1.call-done = bf16[2,64,4,128]{3,2,1,0:T(4,128)(2,1)} async-done(((bf16[2,64,4,128]{3,2,1,0:T(4,128)(2,1)}), bf16[2,64,4,128]{3,2,1,0:T(4,128)(2,1)}) %all-reduce.9.cloned.1.call-update) | async-done | bytes 131088 | tf_op jit(solution)/shard_map/psum | solution.py:99
  988.8 0.9 copy.95
  989.7 0.6 gather_fusion.3
  990.3 0.4 convolution_bitcast_fusion
  991.0 0.9 copy.99
  (44 shorter events, 2.0 us)
Async XLA Ops:
  7.2 354.2 %copy-start = (s32[16]{0:T(128)S(1)}, s32[16]{0:T(128)}, u32[]{:S(2)}) copy-start(s32[16]{0:T(128)} %param.17) | copy-start | bytes 196
  7.2 0.7 copy-start.5
  7.2 348.2 %all-reduce.7.cloned.1.call-start = ((), (), s32[]{:S(2)}) async-start(), calls=%async_computation | async-start | bytes 524288 | tf_op jit(solution)/shard_map/psum | solution.py:88
  68.0 1.0 copy-start.1
  70.6 284.8 %copy-start.3 = (bf16[2,64,512]{2,1,0:T(8,128)(2,1)S(1)}, bf16[2,64,512]{2,1,0:T(8,128)(2,1)}, u32[]{:S(2)}) copy-start(bf16[2,64,512]{2,1,0:T(8,128)(2,1)} %param.12) | copy-start | bytes 393220
  70.6 490.7 %all-reduce.11.cloned.1.call-start = ((), (), s32[]{:S(2)}) async-start(), calls=%async_computation.2 | async-start | bytes 2097152
  359.3 629.4 %all-reduce.9.cloned.1.call-start = ((), (), s32[]{:S(2)}) async-start(), calls=%async_computation.1 | async-start | bytes 262144 | tf_op jit(solution)/shard_map/psum | solution.py:99
  361.3 0.7 copy-start.6
  362.0 199.4 %copy-start.2 = (bf16[2,4,2048]{2,1,0:T(4,128)(2,1)S(1)}, bf16[2,4,2048]{2,1,0:T(4,128)(2,1)}, u32[]{:S(2)}) copy-start(bf16[2,4,2048]{2,1,0:T(4,128)(2,1)} %param.13) | copy-start | bytes 98308
  362.0 199.4 %copy-start.4 = (bf16[2,4,2048]{2,1,0:T(4,128)(2,1)S(1)}, bf16[2,4,2048]{2,1,0:T(4,128)(2,1)}, u32[]{:S(2)}) copy-start(bf16[2,4,2048]{2,1,0:T(4,128)(2,1)} %param.19) | copy-start | bytes 98308
Sparse Core Ops, SparseCore 0:
  70.8 284.5 all-reduce.6
  359.5 201.8 all-reduce.10
  733.1 255.6 all-reduce.8
where the time goes:
time: 999 us; the launch traced here: 998 us
  waiting for transfers between devices  739 us (74%)
  blocking collectives  224 us (22%)
  between operations  15.3 us (2%)
  local copies, waits for them, and re-layouts  10.9 us (1%)
    psum x1, waiting for transfers between devices, local(): fitted = lax.psum(fit_part, 'atom')  285 us
    psum x1, waiting for transfers between devices, local(): grad_resid = lax.psum(back_part.astype(jnp.bfloat16), 'atom')  255 us
    unnamed x4, waiting for transfers between devices  199 us
    psum x1, blocking collectives, local(): threshold_grads = lax.psum(theta_part, ('dof', 'atom'))  119 us
    all_gather x1, blocking collectives, local(): codes_all = lax.all_gather(codes_now, 'dof', axis=1, tiled=True)  58 us
    all_gather x1, blocking collectives, local(): grad_codes = lax.all_gather(grad_share, 'dof', axis=1, tiled=True)  47.3 us
  transfers between devices with their start and end apart: 3, of which 3 were waited for; matrix products, arithmetic and copies ran while one was open for 0% of the time, Pallas kernels for 0%

commit v1 on v0

v1 whole, which is shorter than its diff:
```python
import functools

import jax
import jax.numpy as jnp
from jax import lax
from jax.experimental import pallas as pl
from jax.experimental.pallas import tpu as pltpu
from jax.sharding import PartitionSpec as P

MESH = pl.DeviceIdType.MESH
F32 = jnp.float32
BF16 = jnp.bfloat16
T = 128
V = 8


def swap(x):
    turned = pltpu.roll(x, V // 2, 1)
    rows = lax.broadcasted_iota(jnp.int32, x.shape, 1)
    return jnp.where(rows < V // 2, -turned, turned)


def nt(a, b):
    return lax.dot_general(a, b, (((1,), (1,)), ((), ())), preferred_element_type=F32)


def nn(a, b):
    return lax.dot_general(a, b, (((1,), (0,)), ((), ())), preferred_element_type=F32)


def tn(a, b):
    return lax.dot_general(a, b, (((0,), (0,)), ((), ())), preferred_element_type=F32)


def wait_bytes(ref, sem):
    pltpu.make_async_copy(ref, ref, sem).wait()


def kernel(
    n_dof, n_atom, slots, row_tiles, atom_tiles, groups,
    received, codes, tiles, coords, counts, group_ids, thresholds, cotangent,
    next_out, grads_out, thr_out,
    places, held, shares, rec,
    codes_send, codes_recv, corr_send, corr_recv, grad_send, grad_recv,
    codes_pick, grad_pick,
    part, pair, half, gather, resid, resid_share,
    sized, part_b, pair_b, half_b, gather_b, back, back_share,
    thr_part, thr_dof, thr_sum, thr_pair, thr_both, thr_atom,
    send, recv,
):
    p = lax.axis_index("dof")
    q = lax.axis_index("atom")
    chips = n_atom // 2
    chip, core = q // 2, q % 2
    rows = V * n_dof
    total = row_tiles * rows
    chunk = total // n_atom

    def dof_peer(j):
        return lax.rem(p + j, n_dof)

    def chip_peer(j):
        return lax.rem(chip + j, chips)

    mate = (p, chip * 2 + 1 - core)

    barrier = pltpu.get_barrier_semaphore()

    @pl.loop(1, n_dof)
    def _(j):
        pl.semaphore_signal(barrier, inc=1, device_id=(dof_peer(j), q), device_id_type=MESH)

    @pl.loop(1, chips)
    def _(j):
        pl.semaphore_signal(
            barrier, inc=1, device_id=(p, chip_peer(j) * 2 + core), device_id_type=MESH
        )

    pl.semaphore_signal(barrier, inc=1, device_id=mate, device_id_type=MESH)

    for k in range(atom_tiles):
        cols = slice(k * T, (k + 1) * T)
        held[k] = jnp.concatenate(
            [codes[0, :, cols].astype(F32), codes[1, :, cols].astype(F32)], axis=0
        )
    rec[...] = received[...].astype(F32)

    pl.semaphore_wait(barrier, n_dof - 1 + chips - 1 + 1)

    def remote(src, dst, s, device):
        return pltpu.make_async_remote_copy(
            src_ref=src, dst_ref=dst, send_sem=send.at[s], recv_sem=recv.at[s],
            device_id=device, device_id_type=MESH,
        )

    @pl.loop(1, n_dof)
    def _(j):
        remote(coords, places.at[p], 0, (dof_peer(j), q)).start()

    for l in range(slots):
        places[p, l, 0] = coords[l, 0]
        places[p, l, 1] = coords[l, 1]
    wait_bytes(places.at[pl.ds(0, n_dof - 1)], recv.at[0])

    def hot(flag):
        return jnp.where(flag, 1.0, 0.0).astype(F32)

    live = [hot(l < counts[0, 0]) for l in range(slots)]

    def pick_and_send(table, out, into, s):
        def build(peer):
            return jnp.concatenate(
                [table[places[peer, l, 1]] for l in range(slots)], axis=0
            ).astype(BF16)

        @pl.loop(1, n_dof)
        def _(j):
            peer = dof_peer(j)
            out[peer] = build(peer)
            remote(out.at[peer], into.at[p], s, (peer, q)).start()

        into[p] = build(p)
        wait_bytes(into.at[pl.ds(0, n_dof - 1)], recv.at[s])

    def apply(arrived, picked, dst):
        x = arrived[...].astype(F32)
        products = []
        for l in range(slots):
            xl = x[:, l * V : (l + 1) * V, :]
            plain = xl.reshape(rows, T).astype(BF16)
            turned = swap(xl).reshape(rows, T).astype(BF16)
            picked[l, :, :T] = plain
            picked[l, :, T:] = turned
            products.append(nt(plain, tiles[l, 0]) + nt(turned, tiles[l, 1]))
        for r in range(row_tiles):
            acc = products[0] * (live[0] * hot(coords[0, 0] == r))
            for l in range(1, slots):
                acc += products[l] * (live[l] * hot(coords[l, 0] == r))
            dst[r * rows : (r + 1) * rows, :] = acc.astype(dst.dtype)

    def sum_and_share(dst, pairing, halved, gathered, share, full, finish, s):
        n_half = total // 2
        mine = pl.ds(pl.multiple_of(core * n_half, n_half), n_half)
        theirs = pl.ds(pl.multiple_of((1 - core) * n_half, n_half), n_half)
        remote(dst.at[theirs], pairing, s, mate).start()
        wait_bytes(pairing, recv.at[s])
        halved[...] = (dst[mine, :].astype(F32) + pairing[...].astype(F32)).astype(halved.dtype)

        def rows_of(c):
            return pl.ds(pl.multiple_of(c * chunk, chunk), chunk)

        @pl.loop(1, chips)
        def _(j):
            c = chip_peer(j)
            remote(
                halved.at[rows_of(c)], gathered.at[chip], s + 1, (p, c * 2 + core)
            ).start()

        gathered[chip] = halved[rows_of(chip), :]
        wait_bytes(gathered.at[pl.ds(0, chips - 1)], recv.at[s + 1])
        acc = gathered[0].astype(F32)
        for c in range(1, chips):
            acc += gathered[c].astype(F32)
        share[...] = finish(acc).astype(BF16)
        first = core * n_half + chip * chunk
        full_rows = full.at[
            first // rows, pl.ds(pl.multiple_of(first % rows, chunk), chunk)
        ]
        n_tiles = row_tiles // 2
        full_half = full.at[pl.ds(core * n_tiles, n_tiles)]

        @pl.loop(1, chips)
        def _(j):
            remote(share, full_rows, s + 2, (p, chip_peer(j) * 2 + core)).start()

        full_rows[...] = share[...]
        wait_bytes(sized.at[pl.ds(0, (chips - 1) * chunk)], recv.at[s + 2])
        remote(full_half, full_half, s + 3, mate).start()
        wait_bytes(sized, recv.at[s + 3])

        wait_bytes(dst.at[pl.ds(0, n_half)], send.at[s])
        wait_bytes(gathered.at[pl.ds(0, chips - 1)], send.at[s + 1])
        wait_bytes(sized.at[pl.ds(0, (chips - 1) * chunk)], send.at[s + 2])
        wait_bytes(sized, send.at[s + 3])

    pick_and_send(held, codes_send, codes_recv, 1)
    apply(codes_recv, codes_pick, part)

    def minus_received(acc):
        first = (core * chips + chip) * chunk
        tile, inside = first // rows, first % rows
        snaps = pl.ds(pl.multiple_of(inside // 2, V), chunk // 2)
        cols = pl.ds(pl.multiple_of(tile * T, T), T)
        re, im = rec[0, snaps, cols], rec[1, snaps, cols]
        low = lax.broadcasted_iota(jnp.int32, (V, T), 0) < V // 2
        blocks = []
        for b in range(chunk // (2 * V)):
            a, c = re[b * V : (b + 1) * V], im[b * V : (b + 1) * V]
            blocks.append(jnp.where(low, a, pltpu.roll(c, V // 2, 0)))
            blocks.append(jnp.where(low, pltpu.roll(a, V // 2, 0), c))
        return jnp.concatenate(blocks, axis=0) - acc

    sum_and_share(part, pair, half, gather, resid_share, resid, minus_received, 2)

    def row_block(ref, l):
        return ref[coords[l, 0]]

    corr = []
    for l in range(slots):
        plain = row_block(resid, l)
        turned = (
            swap(plain.astype(F32).reshape(n_dof, V, T)).reshape(rows, T).astype(BF16)
        )
        g = (nn(plain, tiles[l, 0]) - nn(turned, tiles[l, 1])) * live[l]
        corr.append(g.reshape(n_dof, V, T))
    corr_send[...] = jnp.concatenate(corr, axis=1).astype(corr_send.dtype)

    @pl.loop(1, n_dof)
    def _(j):
        peer = dof_peer(j)
        remote(corr_send.at[peer], corr_recv.at[p], 6, (peer, q)).start()

    corr_recv[p] = corr_send[p]
    wait_bytes(corr_recv.at[pl.ds(0, n_dof - 1)], recv.at[6])

    def add_tile(j, acc):
        peer, l = j // slots, j % slots
        at = jnp.full((V, T), places[peer, l, 1], jnp.int32)
        v = corr_recv[peer, pl.ds(pl.multiple_of(l * V, V), V), :].astype(F32)
        return tuple(
            a + jnp.where(at == k, v, 0.0) for k, a in enumerate(acc)
        )

    zero = jnp.zeros((V, T), F32)
    sums = lax.fori_loop(0, n_dof * slots, add_tile, (zero,) * atom_tiles)

    thr = [zero] * groups
    for k in range(atom_tiles):
        cols = slice(k * T, (k + 1) * T)
        field = held[k] + sums[k]
        theta = jnp.full((V, T), thresholds[group_ids[k]], F32)
        cot = jnp.concatenate(
            [cotangent[0, :, cols].astype(F32), cotangent[1, :, cols].astype(F32)], axis=0
        )
        square = field * field
        magnitude = jnp.sqrt(square + pltpu.roll(square, V // 2, 0) + 1e-06)
        most = jnp.maximum(magnitude, theta)
        factor = jnp.maximum(magnitude - theta, 0.0) / most
        shrunk = (field * factor).astype(BF16)
        next_out[0, :, cols] = shrunk[: V // 2]
        next_out[1, :, cols] = shrunk[V // 2 :]
        product = cot * field
        pulled = (product + pltpu.roll(product, V // 2, 0)) / most
        above = jnp.where(magnitude > theta, 1.0, jnp.where(magnitude == theta, 0.5, 0.0))
        pulled = pulled * above
        grad = cot * factor + field * (pulled * (1.0 - factor) / magnitude)
        shares[k] = grad.astype(BF16).astype(F32)
        own = jnp.full((V, T), group_ids[k], jnp.int32)
        thr = [t - jnp.where(own == g, pulled, 0.0) for g, t in enumerate(thr)]

    pick_and_send(shares, grad_send, grad_recv, 7)

    for g in range(groups):
        thr_part[g : g + 1, :] = 0.5 * jnp.sum(thr[g], axis=0, keepdims=True)

    @pl.loop(1, n_dof)
    def _(j):
        remote(thr_part, thr_dof.at[p], 12, (dof_peer(j), q)).start()

    thr_dof[p] = thr_part[...]

    apply(grad_recv, grad_pick, part_b)
    wait_bytes(thr_dof.at[pl.ds(0, n_dof - 1)], recv.at[12])
    acc = thr_dof[0]
    for i in range(1, n_dof):
        acc += thr_dof[i]
    thr_sum[...] = acc
    remote(thr_sum, thr_pair, 13, mate).start()

    sum_and_share(part_b, pair_b, half_b, gather_b, back_share, back, lambda acc: acc, 8)

    wait_bytes(thr_pair, recv.at[13])
    thr_both[...] = thr_sum[...] + thr_pair[...]

    @pl.loop(1, chips)
    def _(j):
        remote(thr_both, thr_atom.at[chip], 14, (p, chip_peer(j) * 2 + core)).start()

    thr_atom[chip] = thr_both[...]

    for l in range(slots):
        left = tn(row_block(resid, l), grad_pick[l])
        right = tn(row_block(back, l), codes_pick[l])
        g = ((left - right) * live[l]).astype(BF16)
        grads_out[l, 0] = g[:, :T]
        grads_out[l, 1] = g[:, T:]

    wait_bytes(thr_atom.at[pl.ds(0, chips - 1)], recv.at[14])
    acc = thr_atom[0]
    for c in range(1, chips):
        acc += thr_atom[c]
    thr_out[...] = jnp.sum(acc, axis=1, keepdims=True)

    wait_bytes(places.at[pl.ds(0, n_dof - 1)], send.at[0])
    wait_bytes(codes_recv.at[pl.ds(0, n_dof - 1)], send.at[1])
    wait_bytes(corr_recv.at[pl.ds(0, n_dof - 1)], send.at[6])
    wait_bytes(grad_recv.at[pl.ds(0, n_dof - 1)], send.at[7])
    wait_bytes(thr_dof.at[pl.ds(0, n_dof - 1)], send.at[12])
    wait_bytes(thr_pair, send.at[13])
    wait_bytes(thr_atom.at[pl.ds(0, chips - 1)], send.at[14])


def local(n_dof, n_atom, received, codes, tiles, coords, counts, group_ids, thresholds, cotangent):
    slots = tiles.shape[2]
    row_tiles = received.shape[2] // T
    atom_tiles = codes.shape[2] // T
    groups = thresholds.shape[0]
    rows = V * n_dof
    total = row_tiles * rows
    chunk = total // n_atom
    chips = n_atom // 2
    vmem = pl.BlockSpec(memory_space=pltpu.VMEM)
    smem = pl.BlockSpec(memory_space=pltpu.SMEM)

    def exchange(dtype):
        return [pltpu.VMEM((n_dof, slots * V, T), dtype)] * 2

    def summing(dtype):
        return [
            pltpu.VMEM((total, T), dtype),
            pltpu.VMEM((total // 2, T), dtype),
            pltpu.VMEM((total // 2, T), dtype),
            pltpu.VMEM((chips, chunk, T), dtype),
            pltpu.VMEM((row_tiles, rows, T), BF16),
            pltpu.VMEM((chunk, T), BF16),
        ]

    out = pl.pallas_call(
        functools.partial(kernel, n_dof, n_atom, slots, row_tiles, atom_tiles, groups),
        out_shape=(
            jax.ShapeDtypeStruct(codes.shape, BF16),
            jax.ShapeDtypeStruct(tiles.shape[2:], BF16),
            jax.ShapeDtypeStruct((groups, 1), F32),
        ),
        in_specs=[vmem, vmem, vmem, smem, smem, smem, smem, vmem],
        out_specs=(vmem, vmem, vmem),
        scratch_shapes=[
            pltpu.SMEM((n_dof, slots, 2), jnp.int32),
            pltpu.VMEM((atom_tiles, V, T), F32),
            pltpu.VMEM((atom_tiles, V, T), F32),
            pltpu.VMEM(received.shape, F32),
            *exchange(BF16),
            *exchange(F32),
            *exchange(BF16),
            pltpu.VMEM((slots, rows, 2 * T), BF16),
            pltpu.VMEM((slots, rows, 2 * T), BF16),
            *summing(F32),
            pltpu.VMEM((total // 2, T), BF16),
            *summing(BF16),
            pltpu.VMEM((groups, T), F32),
            pltpu.VMEM((n_dof, groups, T), F32),
            pltpu.VMEM((groups, T), F32),
            pltpu.VMEM((groups, T), F32),
            pltpu.VMEM((groups, T), F32),
            pltpu.VMEM((chips, groups, T), F32),
            pltpu.SemaphoreType.DMA((15,)),
            pltpu.SemaphoreType.DMA((15,)),
        ],
        compiler_params=pltpu.CompilerParams(
            collective_id=0, has_side_effects=True, vmem_limit_bytes=32 * 1024 * 1024
        ),
    )(received, codes, tiles[0, 0], coords[0, 0], counts, group_ids, thresholds, cotangent)
    codes_next, tile_grads, threshold_grads = out
    return codes_next, tile_grads[None, None], threshold_grads[:, 0]


def solution(mesh):
    placed = (
        P(None, None, "dof"),
        P(None, "dof", "atom"),
        P("dof", "atom", None, None, None, None),
        P("dof", "atom", None, None),
        P("dof", "atom"),
        P("atom"),
        P(),
        P(None, "dof", "atom"),
    )
    return jax.shard_map(
        functools.partial(local, mesh.shape["dof"], mesh.shape["atom"]),
        mesh=mesh,
        in_specs=placed,
        out_specs=(P(None, "dof", "atom"), P("dof", "atom", None, None, None, None), P()),
        check_vma=False,
    )
```

time: 999 us -> 110 us (0.11)
  waiting for transfers between devices: 739 us -> 0 us
  blocking collectives: 224 us -> 0 us
  Pallas kernels: 0 us -> 101 us
  between operations: 15.3 us -> 1.3 us
    psum x2 -> x0, waiting for transfers between devices: 540 us -> none  [the longest x1 285 us: local(): fitted = lax.psum(fit_part, 'atom')]
    unnamed x4 -> x0, waiting for transfers between devices: 199 us -> none
    psum x1 -> x0, blocking collectives: 119 us -> none  [local(): threshold_grads = lax.psum(theta_part, ('dof', 'atom'))]
    all_gather x2 -> x0, blocking collectives: 105 us -> none  [the longest x1 58 us: local(): codes_all = lax.all_gather(codes_now, 'dof', axis=1, tiled=True)]
    pallas_call x0 -> x1, Pallas kernels: none -> 101 us  [local(): pl.pallas_call(functools.partial(kernel, n_dof, n_atom, slots, row_tiles,...]
  transfers between devices with their start and end apart: 3 -> 0, of which waited for: 3 -> 0; matrix products, arithmetic and copies ran while one was open for 0% -> 0% of each run, Pallas kernels for 0% -> 0%
where the time goes in v1:
time: 110 us; the launch traced here: 109 us
  Pallas kernels  101 us (92%)
  local copies, waits for them, and re-layouts  6.03 us (5%)
  between operations  1.3 us (1%)
    pallas_call x1, Pallas kernels, local(): pl.pallas_call(functools.partial(kernel, n_dof, n_atom, slots, row_tiles,...  101 us
    unnamed x16, local copies, waits for them, and re-layouts  5.93 us

profile of v1, /device:TPU:1, one launch (start us, length us, event | category | flops | bytes accessed | tf_op | source)
XLA Modules:
  0.0 109.4 jit_solution(3539018877449997978)
XLA Ops:
  1.3 0.0 copy-start.6
  1.3 0.7 copy-done.6
  2.0 0.0 copy-start.4
  2.0 0.0 copy-start.5
  2.0 0.1 copy.12.coords
  2.1 0.6 copy-done.4
  2.6 0.0 copy-done.5
  2.6 0.0 copy-start
  2.6 0.9 copy-done
  3.6 0.0 copy-start.1
  3.6 0.9 copy-done.1
  4.5 0.0 copy-start.2
  4.5 0.8 copy-done.2
  5.2 0.0 copy-start.3
  5.2 0.8 copy-done.3
  6.0 101.4 %shard_map.103 = (bf16[2,4,2048]{2,1,0:T(4,128)(2,1)S(1)}, bf16[4,2,128,128]{3,2,1,0:T(8,128)(2,1)S(1)}, f32[8,1]{1,0:T(8,128)S(1)}) custom-call(bf16[2,64,512]{2,1,0:T(8,128)(2,1)S(1)} %copy-done.1, bf16[2,4,2048]{2,1,0:T(4,128)(2,1)S(1)} %copy-done.2, bf16[4,2,128,128]{3,2,1,0:T(8,128)(2,1)S(1)} %bitcast.3, s32[4,2]{1,0:T(4,128)S(1)} %copy.12.coords, ...), custom_call_target="tpu_custom_call" | custom-call | tf_op jit(solution)/shard_map/pallas_call | solution.py:338
  107.4 0.6 reduce
  108.1 0.6 copy.16
  108.7 0.7 copy.17
Async XLA Ops:
  1.3 0.7 copy-start.6
  2.0 0.7 copy-start.4
  2.0 0.7 copy-start.5
  2.6 0.9 copy-start
  3.6 0.9 copy-start.1
  4.5 0.8 copy-start.2
  5.2 0.8 copy-start.3

commit v2 on v1

v2 whole, which is shorter than its diff:
```python
import functools

import jax
import jax.numpy as jnp
from jax import lax
from jax.experimental import pallas as pl
from jax.experimental.pallas import tpu as pltpu
from jax.sharding import PartitionSpec as P

MESH = pl.DeviceIdType.MESH
F32 = jnp.float32
BF16 = jnp.bfloat16
T = 128
V = 8


def swap(x):
    turned = pltpu.roll(x, V // 2, 1)
    rows = lax.broadcasted_iota(jnp.int32, x.shape, 1)
    return jnp.where(rows < V // 2, -turned, turned)


def nt(a, b):
    return lax.dot_general(a, b, (((1,), (1,)), ((), ())), preferred_element_type=F32)


def nn(a, b):
    return lax.dot_general(a, b, (((1,), (0,)), ((), ())), preferred_element_type=F32)


def tn(a, b):
    return lax.dot_general(a, b, (((0,), (0,)), ((), ())), preferred_element_type=F32)


def wait_bytes(ref, sem):
    pltpu.make_async_copy(ref, ref, sem).wait()


def entry(values, t):
    out = values[-1]
    for i in reversed(range(len(values) - 1)):
        out = jnp.where(t == i, values[i], out)
    return out


def kernel(
    n_dof, n_atom, slots, row_tiles, atom_tiles, groups,
    received_hbm, codes_hbm, tiles_hbm, coords_hbm, counts_hbm, ids_hbm, thresholds_hbm, cotangent_hbm,
    next_out, grads_out, thr_out,
    received, codes, tiles, cotangent, coords, counts, group_ids, thresholds,
    near, places, held, shares, rec,
    dense, dense_recv, blocks, codes_send, codes_recv,
    corr_send, corr_recv, grad_send, grad_recv, codes_pick, grad_pick,
    part, pair, half, gather, resid, resid_share,
    part_b, gather_b, back, back_share, lefts, sized,
    thr_part, thr_dof, thr_sum, thr_atom,
    send, recv, fetch,
):
    p = lax.axis_index("dof")
    q = lax.axis_index("atom")
    z_hi, z_lo = 4, 4
    ny, nx = n_dof // z_hi, n_atom // (2 * z_lo)
    chips = n_atom // 2
    chip, core = q // 2, q % 2
    y, zh = p // z_hi, p % z_hi
    x, zl = chip // z_lo, chip % z_lo
    rows = V * n_dof
    total = row_tiles * rows
    chunk = total // n_atom
    n_half = total // 2
    away = (2, 1, 3, 0)

    def dof_peer(t):
        dz, dy = entry(away, t // ny), (entry(away, t % ny) if ny > 1 else 0)
        return lax.rem(y + dy, ny) * z_hi + lax.rem(zh + dz, z_hi)

    def chip_peer(t):
        outer = (nx - 1) * z_lo
        dx = jnp.where(t < outer, entry(away[:3], t // z_lo), 0)
        end = jnp.where(zl < z_lo // 2, z_lo - 1 - t % z_lo, t % z_lo)
        to = jnp.where(t < outer, end, lax.rem(zl + t - outer + 1, z_lo))
        return lax.rem(x + dx, nx) * z_lo + to

    mate = (p, chip * 2 + 1 - core)

    fetches = [
        pltpu.make_async_copy(a, b, fetch.at[i])
        for i, (a, b) in enumerate([
            (coords_hbm, coords), (codes_hbm, codes), (tiles_hbm, tiles), (counts_hbm, counts),
            (received_hbm, received), (cotangent_hbm, cotangent), (ids_hbm, group_ids),
            (thresholds_hbm, thresholds),
        ])
    ]
    for f in fetches:
        f.start()

    barrier = pltpu.get_barrier_semaphore()

    def greet(device):
        pl.semaphore_signal(barrier, inc=1, device_id=device, device_id_type=MESH)

    @pl.loop(0, n_dof - 1)
    def _(t):
        greet((dof_peer(t), q))

    @pl.loop(0, chips - 1)
    def _(t):
        c = chip_peer(t)
        greet((p, c * 2))
        greet((p, c * 2 + 1))

    greet(mate)

    fetches[0].wait()
    fetches[1].wait()
    for k in range(atom_tiles):
        cols = slice(k * T, (k + 1) * T)
        tile = jnp.concatenate(
            [codes[0, :, cols].astype(F32), codes[1, :, cols].astype(F32)], axis=0
        )
        held[k] = tile
        blocks[zh, k] = tile
    dense[...] = held[...].reshape(atom_tiles * V, T).astype(BF16)

    pl.semaphore_wait(barrier, n_dof - 1 + n_atom - 1)

    def remote(src, dst, s, device, r=None):
        return pltpu.make_async_remote_copy(
            src_ref=src, dst_ref=dst, send_sem=send.at[s], recv_sem=recv.at[s if r is None else r],
            device_id=device, device_id_type=MESH,
        )

    leaving = []

    for dz in away[:-1]:
        to = lax.rem(zh + dz, z_hi)
        remote(dense, dense_recv.at[zh], 15 + dz, (y * z_hi + to, q), 15 + z_hi - dz).start()
        leaving.append((dense, 15 + dz))
    for dy in range(1, ny):
        to = lax.rem(y + dy, ny)
        remote(coords, near.at[y], 0, (to * z_hi + zh, q)).start()

    @pl.loop(0, n_dof - 1)
    def _(t):
        remote(coords, places.at[p], 1, (dof_peer(t), q)).start()

    leaving.append((places.at[pl.ds(0, n_dof - 1)], 1))
    for l in range(slots):
        for d in range(2):
            near[y, d, l] = coords[d, l]
            places[p, d, l] = coords[d, l]
    if ny > 1:
        wait_bytes(near.at[pl.ds(0, ny - 1)], recv.at[0])
        leaving.append((near.at[pl.ds(0, ny - 1)], 0))

    def build(table, named):
        return jnp.concatenate([table(named(l)) for l in range(slots)], axis=0).astype(BF16)

    for dz in (0, 1, 3, 2):
        z = lax.rem(zh + dz, z_hi)
        if dz:
            wait_bytes(dense_recv.at[z], recv.at[15 + dz])
            blocks[z] = dense_recv[z].astype(F32).reshape(atom_tiles, V, T)
        for dy in range(1, ny):
            to = lax.rem(y + dy, ny)
            codes_send[to, z] = build(lambda k, z=z: blocks[z, k], lambda l, to=to: near[to, 1, l])
            remote(codes_send.at[to, z], codes_recv.at[y * z_hi + z], 2, (to * z_hi + zh, q)).start()
        codes_recv[y * z_hi + z] = build(lambda k, z=z: blocks[z, k], lambda l: coords[1, l])
    fetches[2].wait()
    fetches[3].wait()
    fetches[4].wait()
    rec[...] = received[...].astype(F32)
    if ny > 1:
        wait_bytes(codes_recv.at[pl.ds(0, (ny - 1) * z_hi)], recv.at[2])
        leaving.append((codes_recv.at[pl.ds(0, (ny - 1) * z_hi)], 2))

    def hot(flag):
        return jnp.where(flag, 1.0, 0.0).astype(F32)

    live = [hot(l < counts[0, 0]) for l in range(slots)]

    def apply(arrived, picked, dst):
        v = arrived[...].astype(F32)
        products = []
        for l in range(slots):
            xl = v[:, l * V : (l + 1) * V, :]
            plain = xl.reshape(rows, T).astype(BF16)
            turned = swap(xl).reshape(rows, T).astype(BF16)
            picked[l, :, :T] = plain
            picked[l, :, T:] = turned
            products.append(nt(plain, tiles[l, 0]) + nt(turned, tiles[l, 1]))
        for r in range(row_tiles):
            acc = products[0] * (live[0] * hot(coords[0, 0] == r))
            for l in range(1, slots):
                acc += products[l] * (live[l] * hot(coords[0, l] == r))
            dst[r * rows : (r + 1) * rows, :] = acc.astype(dst.dtype)

    def rows_of(c):
        return pl.ds(pl.multiple_of(c * chunk, chunk), chunk)

    def to_all(make):
        @pl.loop(0, chips - 1)
        def _(t):
            c = chip_peer(t)
            for k in range(2):
                make(c, k).start()

        make(chip, 1 - core).start()

    def share_all(share, full, s):
        first = core * n_half + chip * chunk
        place = full.at[first // rows, pl.ds(pl.multiple_of(first % rows, chunk), chunk)]
        to_all(lambda c, k: remote(share, place, s, (p, c * 2 + k)))
        place[...] = share[...]
        leaving.append((sized.at[pl.ds(0, total - chunk)], s))

    apply(codes_recv, codes_pick, part)
    mine = pl.ds(pl.multiple_of(core * n_half, n_half), n_half)
    theirs = pl.ds(pl.multiple_of((1 - core) * n_half, n_half), n_half)
    remote(part.at[theirs], pair, 3, mate).start()
    wait_bytes(pair, recv.at[3])
    leaving.append((pair, 3))
    half[...] = part[mine, :] + pair[...]

    @pl.loop(0, chips - 1)
    def _(t):
        c = chip_peer(t)
        remote(half.at[rows_of(c)], gather.at[chip], 4, (p, c * 2 + core)).start()

    gather[chip] = half[rows_of(chip), :]
    wait_bytes(gather.at[pl.ds(0, chips - 1)], recv.at[4])
    leaving.append((gather.at[pl.ds(0, chips - 1)], 4))
    acc = gather[0]
    for c in range(1, chips):
        acc += gather[c]

    first = (core * chips + chip) * chunk
    snaps = pl.ds(pl.multiple_of(first % rows // 2, V), chunk // 2)
    cols = pl.ds(pl.multiple_of(first // rows * T, T), T)
    re, im = rec[0, snaps, cols], rec[1, snaps, cols]
    low = lax.broadcasted_iota(jnp.int32, (V, T), 0) < V // 2
    ordered = []
    for b in range(chunk // (2 * V)):
        a, c = re[b * V : (b + 1) * V], im[b * V : (b + 1) * V]
        ordered.append(jnp.where(low, a, pltpu.roll(c, V // 2, 0)))
        ordered.append(jnp.where(low, pltpu.roll(a, V // 2, 0), c))
    resid_share[...] = (jnp.concatenate(ordered, axis=0) - acc).astype(BF16)
    share_all(resid_share, resid, 5)
    wait_bytes(sized.at[pl.ds(0, total - chunk)], recv.at[5])

    def row_block(ref, l):
        return ref[coords[0, l]]

    corr = []
    for l in range(slots):
        plain = row_block(resid, l)
        turned = swap(plain.astype(F32).reshape(n_dof, V, T)).reshape(rows, T).astype(BF16)
        g = (nn(plain, tiles[l, 0]) - nn(turned, tiles[l, 1])) * live[l]
        corr.append(g.reshape(n_dof, V, T))
    corr_send[...] = jnp.concatenate(corr, axis=1).astype(corr_send.dtype)

    @pl.loop(0, n_dof - 1)
    def _(t):
        peer = dof_peer(t)
        remote(corr_send.at[peer], corr_recv.at[p], 6, (peer, q)).start()

    leaving.append((corr_recv.at[pl.ds(0, n_dof - 1)], 6))
    corr_recv[p] = corr_send[p]
    fetches[5].wait()
    fetches[6].wait()
    fetches[7].wait()
    wait_bytes(places.at[pl.ds(0, n_dof - 1)], recv.at[1])
    wait_bytes(corr_recv.at[pl.ds(0, n_dof - 1)], recv.at[6])

    def add_tile(j, acc):
        peer, l = j // slots, j % slots
        at = jnp.full((V, T), places[peer, 1, l], jnp.int32)
        v = corr_recv[peer, pl.ds(pl.multiple_of(l * V, V), V), :].astype(F32)
        return tuple(a + jnp.where(at == k, v, 0.0) for k, a in enumerate(acc))

    zero = jnp.zeros((V, T), F32)
    sums = lax.fori_loop(0, n_dof * slots, add_tile, (zero,) * atom_tiles)

    thr = [zero] * groups
    for k in range(atom_tiles):
        cols = slice(k * T, (k + 1) * T)
        field = held[k] + sums[k]
        theta = jnp.full((V, T), thresholds[group_ids[k]], F32)
        cot = jnp.concatenate(
            [cotangent[0, :, cols].astype(F32), cotangent[1, :, cols].astype(F32)], axis=0
        )
        square = field * field
        magnitude = jnp.sqrt(square + pltpu.roll(square, V // 2, 0) + 1e-06)
        most = jnp.maximum(magnitude, theta)
        factor = jnp.maximum(magnitude - theta, 0.0) / most
        shrunk = (field * factor).astype(BF16)
        next_out[0, :, cols] = shrunk[: V // 2]
        next_out[1, :, cols] = shrunk[V // 2 :]
        product = cot * field
        pulled = (product + pltpu.roll(product, V // 2, 0)) / most
        above = jnp.where(magnitude > theta, 1.0, jnp.where(magnitude == theta, 0.5, 0.0))
        pulled = pulled * above
        grad = cot * factor + field * (pulled * (1.0 - factor) / magnitude)
        shares[k] = grad.astype(BF16).astype(F32)
        own = jnp.full((V, T), group_ids[k], jnp.int32)
        thr = [t - jnp.where(own == g, pulled, 0.0) for g, t in enumerate(thr)]

    @pl.loop(0, n_dof - 1)
    def _(t):
        peer = dof_peer(t)
        grad_send[peer] = build(lambda k: shares[k], lambda l: places[peer, 1, l])
        remote(grad_send.at[peer], grad_recv.at[p], 7, (peer, q)).start()

    leaving.append((grad_recv.at[pl.ds(0, n_dof - 1)], 7))
    grad_recv[p] = build(lambda k: shares[k], lambda l: coords[1, l])

    lanes = lax.broadcasted_iota(jnp.int32, (1, T), 1)
    row = jnp.zeros((1, T), F32)
    for g in range(groups):
        row = jnp.where(lanes == g, 0.5 * jnp.sum(thr[g]), row)
    thr_part[...] = row

    @pl.loop(0, n_dof - 1)
    def _(t):
        remote(thr_part, thr_dof.at[p], 8, (dof_peer(t), q)).start()

    leaving.append((thr_dof.at[pl.ds(0, n_dof - 1)], 8))
    thr_dof[p] = thr_part[...]
    wait_bytes(grad_recv.at[pl.ds(0, n_dof - 1)], recv.at[7])

    apply(grad_recv, grad_pick, part_b)
    to_all(
        lambda c, k: remote(
            part_b.at[rows_of(k * chips + c)], gather_b.at[q], 9, (p, c * 2 + k)
        )
    )
    leaving.append((gather_b.at[pl.ds(0, n_atom - 1)], 9))
    gather_b[q] = part_b[rows_of(core * chips + chip), :]
    for l in range(slots):
        lefts[l] = tn(row_block(resid, l), grad_pick[l])
    wait_bytes(gather_b.at[pl.ds(0, n_atom - 1)], recv.at[9])
    acc = gather_b[0].astype(F32)
    for c in range(1, n_atom):
        acc += gather_b[c].astype(F32)
    back_share[...] = acc.astype(BF16)
    share_all(back_share, back, 10)

    wait_bytes(thr_dof.at[pl.ds(0, n_dof - 1)], recv.at[8])
    row = thr_dof[0]
    for i in range(1, n_dof):
        row += thr_dof[i]
    thr_sum[...] = row
    to_all(lambda c, k: remote(thr_sum, thr_atom.at[q], 11, (p, c * 2 + k)))
    leaving.append((thr_atom.at[pl.ds(0, n_atom - 1)], 11))
    thr_atom[q] = row

    wait_bytes(sized.at[pl.ds(0, total - chunk)], recv.at[10])
    for l in range(slots):
        right = tn(row_block(back, l), codes_pick[l])
        g = ((lefts[l] - right) * live[l]).astype(BF16)
        grads_out[l, 0] = g[:, :T]
        grads_out[l, 1] = g[:, T:]

    wait_bytes(thr_atom.at[pl.ds(0, n_atom - 1)], recv.at[11])
    row = thr_atom[0]
    for c in range(1, n_atom):
        row += thr_atom[c]
    thr_out[...] = row

    for ref, s in leaving:
        wait_bytes(ref, send.at[s])


def local(n_dof, n_atom, received, codes, tiles, coords, counts, group_ids, thresholds, cotangent):
    slots = tiles.shape[2]
    row_tiles = received.shape[2] // T
    atom_tiles = codes.shape[2] // T
    groups = thresholds.shape[0]
    rows = V * n_dof
    total = row_tiles * rows
    chunk = total // n_atom
    chips = n_atom // 2
    z_hi = 4
    vmem = pl.BlockSpec(memory_space=pltpu.VMEM)
    hbm = pl.BlockSpec(memory_space=pltpu.HBM)

    out = pl.pallas_call(
        functools.partial(kernel, n_dof, n_atom, slots, row_tiles, atom_tiles, groups),
        out_shape=(
            jax.ShapeDtypeStruct(codes.shape, BF16),
            jax.ShapeDtypeStruct(tiles.shape[2:], BF16),
            jax.ShapeDtypeStruct((1, T), F32),
        ),
        in_specs=[hbm] * 8,
        out_specs=(vmem, vmem, vmem),
        scratch_shapes=[
            pltpu.VMEM(received.shape, BF16),
            pltpu.VMEM(codes.shape, BF16),
            pltpu.VMEM(tiles.shape[2:], BF16),
            pltpu.VMEM(codes.shape, BF16),
            pltpu.SMEM((2, slots), jnp.int32),
            pltpu.SMEM(counts.shape, jnp.int32),
            pltpu.SMEM(group_ids.shape, jnp.int32),
            pltpu.SMEM(thresholds.shape, F32),
            pltpu.SMEM((n_dof // z_hi, 2, slots), jnp.int32),
            pltpu.SMEM((n_dof, 2, slots), jnp.int32),
            pltpu.VMEM((atom_tiles, V, T), F32),
            pltpu.VMEM((atom_tiles, V, T), F32),
            pltpu.VMEM(received.shape, F32),
            pltpu.VMEM((atom_tiles * V, T), BF16),
            pltpu.VMEM((z_hi, atom_tiles * V, T), BF16),
            pltpu.VMEM((z_hi, atom_tiles, V, T), F32),
            pltpu.VMEM((n_dof // z_hi, z_hi, slots * V, T), BF16),
            pltpu.VMEM((n_dof, slots * V, T), BF16),
            pltpu.VMEM((n_dof, slots * V, T), F32),
            pltpu.VMEM((n_dof, slots * V, T), F32),
            pltpu.VMEM((n_dof, slots * V, T), BF16),
            pltpu.VMEM((n_dof, slots * V, T), BF16),
            pltpu.VMEM((slots, rows, 2 * T), BF16),
            pltpu.VMEM((slots, rows, 2 * T), BF16),
            pltpu.VMEM((total, T), F32),
            pltpu.VMEM((total // 2, T), F32),
            pltpu.VMEM((total // 2, T), F32),
            pltpu.VMEM((chips, chunk, T), F32),
            pltpu.VMEM((row_tiles, rows, T), BF16),
            pltpu.VMEM((chunk, T), BF16),
            pltpu.VMEM((total, T), BF16),
            pltpu.VMEM((n_atom, chunk, T), BF16),
            pltpu.VMEM((row_tiles, rows, T), BF16),
            pltpu.VMEM((chunk, T), BF16),
            pltpu.VMEM((slots, T, 2 * T), F32),
            pltpu.VMEM((total, T), BF16),
            pltpu.VMEM((1, T), F32),
            pltpu.VMEM((n_dof, 1, T), F32),
            pltpu.VMEM((1, T), F32),
            pltpu.VMEM((n_atom, 1, T), F32),
            pltpu.SemaphoreType.DMA((19,)),
            pltpu.SemaphoreType.DMA((19,)),
            pltpu.SemaphoreType.DMA((8,)),
        ],
        compiler_params=pltpu.CompilerParams(
            collective_id=0, has_side_effects=True, vmem_limit_bytes=62 * 1024 * 1024
        ),
    )(received, codes, tiles[0, 0], coords[0, 0].T, counts, group_ids, thresholds, cotangent)
    codes_next, tile_grads, threshold_grads = out
    return codes_next, tile_grads[None, None], threshold_grads[0, :groups]


def solution(mesh):
    placed = (
        P(None, None, "dof"),
        P(None, "dof", "atom"),
        P("dof", "atom", None, None, None, None),
        P("dof", "atom", None, None),
        P("dof", "atom"),
        P("atom"),
        P(),
        P(None, "dof", "atom"),
    )
    return jax.shard_map(
        functools.partial(local, mesh.shape["dof"], mesh.shape["atom"]),
        mesh=mesh,
        in_specs=placed,
        out_specs=(P(None, "dof", "atom"), P("dof", "atom", None, None, None, None), P()),
        check_vma=False,
    )
```

time: 110 us -> 89.1 us (0.81)
  Pallas kernels: 101 us -> 83.3 us
  local copies, waits for them, and re-layouts: 6.03 us -> 4.23 us
    pallas_call x1, Pallas kernels: 101 us -> 83.3 us  [local(): pl.pallas_call(functools.partial(kernel, n_dof, n_atom, slots, row_tiles,...]
    unnamed x16 -> x4, local copies, waits for them, and re-layouts: 5.93 us -> 3.72 us
where the time goes in v2:
time: 89.1 us; the launch traced here: 88.8 us
  Pallas kernels  83.3 us (93%)
  local copies, waits for them, and re-layouts  4.23 us (5%)
  between operations  1.3 us (1%)
    pallas_call x1, Pallas kernels, local(): pl.pallas_call(functools.partial(kernel, n_dof, n_atom, slots, row_tiles,...  83.3 us
    unnamed x4, local copies, waits for them, and re-layouts  3.72 us

profile of v2, /device:TPU:1, one launch (start us, length us, event | category | flops | bytes accessed | tf_op | source)
XLA Modules:
  0.0 88.8 jit_solution(13539702351879621324)
XLA Ops:
  1.3 83.3 %shard_map.103 = (bf16[2,4,2048]{2,1,0:T(4,128)(2,1)}, bf16[4,2,128,128]{3,2,1,0:T(8,128)(2,1)}, f32[1,128]{1,0:T(1,128)}) custom-call(bf16[2,64,512]{2,1,0:T(8,128)(2,1)} %received_hbm.1, bf16[2,4,2048]{2,1,0:T(4,128)(2,1)} %codes_hbm.1, bf16[4,2,128,128]{3,2,1,0:T(8,128)(2,1)} %bitcast.7, s32[2,4]{1,0:T(2,128)} %bitcast.9, s32[1,1]{1,0:T(1,128)S(6)} %copy.13.counts_hbm, ...), custom_call_target="tpu_custom_call" | custom-call | tf_op jit(solution)/shard_map/pallas_call | solution.py:387
  84.6 0.0 copy-start
  84.6 0.7 copy-done
  85.3 0.5 slice_bitcast_fusion
  85.8 1.4 %copy.14 = bf16[2,4,2048]{2,1,0:T(4,128)(2,1)} copy(bf16[2,4,2048]{2,1,0:T(4,128)(2,1)} %get-tuple-element.12) | data formatting | bytes 65536
  87.2 1.7 %copy.15 = bf16[1,1,4,2,128,128]{5,4,3,2,1,0:T(8,128)(2,1)} copy(bf16[1,1,4,2,128,128]{5,4,3,2,1,0:T(8,128)(2,1)} %bitcast.8) | data formatting | bytes 524288
Async XLA Ops:
  84.6 0.7 copy-start

commit v3 on v2

--- a/solution.py
+++ b/solution.py
@@ -10,6 +10,7 @@
 MESH = pl.DeviceIdType.MESH
 F32 = jnp.float32
 BF16 = jnp.bfloat16
+STEPS = 32000.0
 T = 128
 V = 8
 
@@ -48,13 +49,13 @@
     received_hbm, codes_hbm, tiles_hbm, coords_hbm, counts_hbm, ids_hbm, thresholds_hbm, cotangent_hbm,
     next_out, grads_out, thr_out,
     received, codes, tiles, cotangent, coords, counts, group_ids, thresholds,
-    near, places, held, shares, rec,
+    near, places, held, shares, rec, next_kept, grads_kept,
     dense, dense_recv, blocks, codes_send, codes_recv,
-    corr_send, corr_recv, grad_send, grad_recv, codes_pick, grad_pick,
+    corr_send, corr_recv, scale_send, scale_recv, grad_send, grad_recv, codes_pick, grad_pick,
     part, pair, half, gather, resid, resid_share,
     part_b, gather_b, back, back_share, lefts, sized,
     thr_part, thr_dof, thr_sum, thr_atom,
-    send, recv, fetch,
+    send, recv, fetch, store,
 ):
     p = lax.axis_index("dof")
     q = lax.axis_index("atom")
@@ -257,29 +258,38 @@
         turned = swap(plain.astype(F32).reshape(n_dof, V, T)).reshape(rows, T).astype(BF16)
         g = (nn(plain, tiles[l, 0]) - nn(turned, tiles[l, 1])) * live[l]
         corr.append(g.reshape(n_dof, V, T))
-    corr_send[...] = jnp.concatenate(corr, axis=1).astype(corr_send.dtype)
+    corr = jnp.concatenate(corr, axis=1)
+    most = jnp.maximum(jnp.max(jnp.abs(corr), axis=1, keepdims=True), 1e-30)
+    corr_send[...] = jnp.round(corr * (STEPS / most)).astype(jnp.int32).astype(jnp.int16)
+    scale_send[...] = most * (1.0 / STEPS)
 
     @pl.loop(0, n_dof - 1)
     def _(t):
         peer = dof_peer(t)
         remote(corr_send.at[peer], corr_recv.at[p], 6, (peer, q)).start()
+        remote(scale_send.at[peer], scale_recv.at[p], 12, (peer, q)).start()
 
     leaving.append((corr_recv.at[pl.ds(0, n_dof - 1)], 6))
+    leaving.append((scale_recv.at[pl.ds(0, n_dof - 1)], 12))
     corr_recv[p] = corr_send[p]
+    scale_recv[p] = scale_send[p]
     fetches[5].wait()
     fetches[6].wait()
     fetches[7].wait()
     wait_bytes(places.at[pl.ds(0, n_dof - 1)], recv.at[1])
     wait_bytes(corr_recv.at[pl.ds(0, n_dof - 1)], recv.at[6])
-
-    def add_tile(j, acc):
-        peer, l = j // slots, j % slots
-        at = jnp.full((V, T), places[peer, 1, l], jnp.int32)
-        v = corr_recv[peer, pl.ds(pl.multiple_of(l * V, V), V), :].astype(F32)
-        return tuple(a + jnp.where(at == k, v, 0.0) for k, a in enumerate(acc))
+    wait_bytes(scale_recv.at[pl.ds(0, n_dof - 1)], recv.at[12])
+
+    def add_tiles(peer, acc):
+        tiles_in = corr_recv[peer].astype(jnp.int32).astype(F32) * scale_recv[peer]
+        for l in range(slots):
+            at = jnp.full((V, T), places[peer, 1, l], jnp.int32)
+            v = tiles_in[l * V : (l + 1) * V]
+            acc = tuple(a + jnp.where(at == k, v, 0.0) for k, a in enumerate(acc))
+        return acc
 
     zero = jnp.zeros((V, T), F32)
-    sums = lax.fori_loop(0, n_dof * slots, add_tile, (zero,) * atom_tiles)
+    sums = lax.fori_loop(0, n_dof, add_tiles, (zero,) * atom_tiles)
 
     thr = [zero] * groups
     for k in range(atom_tiles):
@@ -294,8 +304,8 @@
         most = jnp.maximum(magnitude, theta)
         factor = jnp.maximum(magnitude - theta, 0.0) / most
         shrunk = (field * factor).astype(BF16)
-        next_out[0, :, cols] = shrunk[: V // 2]
-        next_out[1, :, cols] = shrunk[V // 2 :]
+        next_kept[0, :, cols] = shrunk[: V // 2]
+        next_kept[1, :, cols] = shrunk[V // 2 :]
         product = cot * field
         pulled = (product + pltpu.roll(product, V // 2, 0)) / most
         above = jnp.where(magnitude > theta, 1.0, jnp.where(magnitude == theta, 0.5, 0.0))
@@ -304,6 +314,9 @@
         shares[k] = grad.astype(BF16).astype(F32)
         own = jnp.full((V, T), group_ids[k], jnp.int32)
         thr = [t - jnp.where(own == g, pulled, 0.0) for g, t in enumerate(thr)]
+
+    stores = [pltpu.make_async_copy(next_kept, next_out, fetch.at[1])]
+    stores[0].start()
 
     @pl.loop(0, n_dof - 1)
     def _(t):
@@ -358,17 +371,37 @@
     for l in range(slots):
         right = tn(row_block(back, l), codes_pick[l])
         g = ((lefts[l] - right) * live[l]).astype(BF16)
-        grads_out[l, 0] = g[:, :T]
-        grads_out[l, 1] = g[:, T:]
+        grads_kept[l, 0] = g[:, :T]
+        grads_kept[l, 1] = g[:, T:]
+        stores.append(pltpu.make_async_copy(grads_kept.at[l], grads_out.at[l], store.at[l]))
+        stores[-1].start()
 
     wait_bytes(thr_atom.at[pl.ds(0, n_atom - 1)], recv.at[11])
     row = thr_atom[0]
     for c in range(1, n_atom):
         row += thr_atom[c]
-    thr_out[...] = row
-
+    for g in range(groups):
+        thr_out[g] = jnp.sum(jnp.where(lanes == g, row, 0.0))
+
+    for copy in stores:
+        copy.wait()
     for ref, s in leaving:
         wait_bytes(ref, send.at[s])
+
+
+def hand_over(a, b, c, a_out, b_out, c_out, a_kept, b_kept, c_kept, sem):
+    n = b.shape[0]
+    parts = [(b.at[l], b_kept.at[l], b_out.at[l]) for l in range(n)]
+    parts += [(a, a_kept, a_out), (c, c_kept, c_out)]
+    loads = [pltpu.make_async_copy(x, k, sem.at[0, i]) for i, (x, k, _) in enumerate(parts)]
+    stores = [pltpu.make_async_copy(k, y, sem.at[1, i]) for i, (_, k, y) in enumerate(parts)]
+    for copy in loads:
+        copy.start()
+    for load, copy in zip(loads, stores):
+        load.wait()
+        copy.start()
+    for copy in stores:
+        copy.wait()
 
 
 def local(n_dof, n_atom, received, codes, tiles, coords, counts, group_ids, thresholds, cotangent):
@@ -381,7 +414,6 @@
     chunk = total // n_atom
     chips = n_atom // 2
     z_hi = 4
-    vmem = pl.BlockSpec(memory_space=pltpu.VMEM)
     hbm = pl.BlockSpec(memory_space=pltpu.HBM)
 
     out = pl.pallas_call(
@@ -389,10 +421,10 @@
         out_shape=(
             jax.ShapeDtypeStruct(codes.shape, BF16),
             jax.ShapeDtypeStruct(tiles.shape[2:], BF16),
-            jax.ShapeDtypeStruct((1, T), F32),
+            jax.ShapeDtypeStruct((groups,), F32),
         ),
         in_specs=[hbm] * 8,
-        out_specs=(vmem, vmem, vmem),
+        out_specs=(hbm, hbm, pl.BlockSpec(memory_space=pltpu.SMEM)),
         scratch_shapes=[
             pltpu.VMEM(received.shape, BF16),
             pltpu.VMEM(codes.shape, BF16),
@@ -407,13 +439,17 @@
             pltpu.VMEM((atom_tiles, V, T), F32),
             pltpu.VMEM((atom_tiles, V, T), F32),
             pltpu.VMEM(received.shape, F32),
+            pltpu.VMEM(codes.shape, BF16),
+            pltpu.VMEM(tiles.shape[2:], BF16),
             pltpu.VMEM((atom_tiles * V, T), BF16),
             pltpu.VMEM((z_hi, atom_tiles * V, T), BF16),
             pltpu.VMEM((z_hi, atom_tiles, V, T), F32),
             pltpu.VMEM((n_dof // z_hi, z_hi, slots * V, T), BF16),
             pltpu.VMEM((n_dof, slots * V, T), BF16),
-            pltpu.VMEM((n_dof, slots * V, T), F32),
-            pltpu.VMEM((n_dof, slots * V, T), F32),
+            pltpu.VMEM((n_dof, slots * V, T), jnp.int16),
+            pltpu.VMEM((n_dof, slots * V, T), jnp.int16),
+            pltpu.VMEM((n_dof, 1, T), F32),
+            pltpu.VMEM((n_dof, 1, T), F32),
             pltpu.VMEM((n_dof, slots * V, T), BF16),
             pltpu.VMEM((n_dof, slots * V, T), BF16),
             pltpu.VMEM((slots, rows, 2 * T), BF16),
@@ -437,13 +473,26 @@
             pltpu.SemaphoreType.DMA((19,)),
             pltpu.SemaphoreType.DMA((19,)),
             pltpu.SemaphoreType.DMA((8,)),
+            pltpu.SemaphoreType.DMA((slots,)),
         ],
         compiler_params=pltpu.CompilerParams(
             collective_id=0, has_side_effects=True, vmem_limit_bytes=62 * 1024 * 1024
         ),
     )(received, codes, tiles[0, 0], coords[0, 0].T, counts, group_ids, thresholds, cotangent)
-    codes_next, tile_grads, threshold_grads = out
-    return codes_next, tile_grads[None, None], threshold_grads[0, :groups]
+    codes_next, tile_grads, threshold_grads = pl.pallas_call(
+        hand_over,
+        out_shape=tuple(jax.ShapeDtypeStruct(o.shape, o.dtype) for o in out),
+        in_specs=[hbm] * 3,
+        out_specs=(hbm,) * 3,
+        scratch_shapes=[
+            pltpu.VMEM(codes.shape, BF16),
+            pltpu.VMEM(tiles.shape[2:], BF16),
+            pltpu.SMEM((groups,), F32),
+            pltpu.SemaphoreType.DMA((2, slots + 2)),
+        ],
+        compiler_params=pltpu.CompilerParams(vmem_limit_bytes=62 * 1024 * 1024),
+    )(*out)
+    return codes_next, tile_grads[None, None], threshold_grads
 
 
 def solution(mesh):

time: 89.1 us -> 80.8 us (0.907)
  local copies, waits for them, and re-layouts: 4.23 us -> 0 us
  Pallas kernels: 83.3 us -> 79.3 us
    pallas_call x1, Pallas kernels: 83.3 us -> 77.6 us  [local(): pl.pallas_call(functools.partial(kernel, n_dof, n_atom, slots, row_tiles,...]
    unnamed x4 -> x0, local copies, waits for them, and re-layouts: 3.72 us -> none
    pallas_call x0 -> x1, Pallas kernels: none -> 1.68 us  [local(): pl.pallas_call(hand_over, out_shape=tuple((jax.ShapeDtypeStruct(o.shape,...]
where the time goes in v3:
time: 80.8 us; the launch traced here: 80.6 us
  Pallas kernels  79.3 us (98%)
  between operations  1.29 us (2%)
    pallas_call x1, Pallas kernels, local(): pl.pallas_call(functools.partial(kernel, n_dof, n_atom, slots, row_tiles,...  77.6 us
    pallas_call x1, Pallas kernels, local(): pl.pallas_call(hand_over, out_shape=tuple((jax.ShapeDtypeStruct(o.shape,...  1.68 us

profile of v3, /device:TPU:1, one launch (start us, length us, event | category | flops | bytes accessed | tf_op | source)
XLA Modules:
  0.0 80.6 jit_solution(889649763271275902)
XLA Ops:
  1.3 77.6 %shard_map.103 = (bf16[2,4,2048]{2,1,0:T(4,128)(2,1)}, bf16[4,2,128,128]{3,2,1,0:T(8,128)(2,1)}, f32[8]{0:T(128)}) custom-call(bf16[2,64,512]{2,1,0:T(8,128)(2,1)} %received_hbm.1, bf16[2,4,2048]{2,1,0:T(4,128)(2,1)} %codes_hbm.1, bf16[4,2,128,128]{3,2,1,0:T(8,128)(2,1)} %bitcast.5, s32[2,4]{1,0:T(2,128)} %bitcast.6, s32[1,1]{1,0:T(1,128)S(6)} %copy.11.counts_hbm, ...), custom_call_target="tpu_custom_call" | custom-call | tf_op jit(solution)/shard_map/pallas_call | solution.py:419
  78.9 1.7 %shard_map.104 = (bf16[2,4,2048]{2,1,0:T(4,128)(2,1)}, bf16[4,2,128,128]{3,2,1,0:T(8,128)(2,1)}, f32[8]{0:T(128)}) custom-call(bf16[2,4,2048]{2,1,0:T(4,128)(2,1)} %get-tuple-element.9.a, bf16[4,2,128,128]{3,2,1,0:T(8,128)(2,1)} %get-tuple-element.10.b, f32[8]{0:T(128)} %get-tuple-element.11.c), custom_call_target="tpu_custom_call" | custom-call | tf_op jit(solution)/shard_map/pallas_call | solution.py:482

commit v4 on v3

--- a/solution.py
+++ b/solution.py
@@ -52,7 +52,7 @@
     near, places, held, shares, rec, next_kept, grads_kept,
     dense, dense_recv, blocks, codes_send, codes_recv,
     corr_send, corr_recv, scale_send, scale_recv, grad_send, grad_recv, codes_pick, grad_pick,
-    part, pair, half, gather, resid, resid_share,
+    part, part_scale, gather, gather_scale, resid, resid_share,
     part_b, gather_b, back, back_share, lefts, sized,
     thr_part, thr_dof, thr_sum, thr_atom,
     send, recv, fetch, store,
@@ -92,17 +92,15 @@
             (thresholds_hbm, thresholds),
         ])
     ]
-    for f in fetches:
-        f.start()
-
     barrier = pltpu.get_barrier_semaphore()
 
     def greet(device):
         pl.semaphore_signal(barrier, inc=1, device_id=device, device_id_type=MESH)
 
-    @pl.loop(0, n_dof - 1)
-    def _(t):
-        greet((dof_peer(t), q))
+    for dz in away[:-1]:
+        greet((y * z_hi + lax.rem(zh + dz, z_hi), q))
+    for dy in range(1, ny):
+        greet((lax.rem(y + dy, ny) * z_hi + zh, q))
 
     @pl.loop(0, chips - 1)
     def _(t):
@@ -111,6 +109,9 @@
         greet((p, c * 2 + 1))
 
     greet(mate)
+
+    for f in fetches:
+        f.start()
 
     fetches[0].wait()
     fetches[1].wait()
@@ -123,7 +124,7 @@
         blocks[zh, k] = tile
     dense[...] = held[...].reshape(atom_tiles * V, T).astype(BF16)
 
-    pl.semaphore_wait(barrier, n_dof - 1 + n_atom - 1)
+    pl.semaphore_wait(barrier, z_hi - 1 + ny - 1 + n_atom - 1)
 
     def remote(src, dst, s, device, r=None):
         return pltpu.make_async_remote_copy(
@@ -141,11 +142,6 @@
         to = lax.rem(y + dy, ny)
         remote(coords, near.at[y], 0, (to * z_hi + zh, q)).start()
 
-    @pl.loop(0, n_dof - 1)
-    def _(t):
-        remote(coords, places.at[p], 1, (dof_peer(t), q)).start()
-
-    leaving.append((places.at[pl.ds(0, n_dof - 1)], 1))
     for l in range(slots):
         for d in range(2):
             near[y, d, l] = coords[d, l]
@@ -175,12 +171,23 @@
         wait_bytes(codes_recv.at[pl.ds(0, (ny - 1) * z_hi)], recv.at[2])
         leaving.append((codes_recv.at[pl.ds(0, (ny - 1) * z_hi)], 2))
 
+    @pl.loop(0, n_dof - 1)
+    def _(t):
+        remote(coords, places.at[p], 1, (dof_peer(t), q)).start()
+
+    leaving.append((places.at[pl.ds(0, n_dof - 1)], 1))
+
     def hot(flag):
         return jnp.where(flag, 1.0, 0.0).astype(F32)
 
     live = [hot(l < counts[0, 0]) for l in range(slots)]
 
-    def apply(arrived, picked, dst):
+    def in_steps(v, axis):
+        most = jnp.maximum(jnp.max(jnp.abs(v), axis=axis, keepdims=True), 1e-30)
+        steps = jnp.round(v * (STEPS / most)).astype(jnp.int32).astype(jnp.int16)
+        return steps, most * (1.0 / STEPS)
+
+    def apply(arrived, picked, put):
         v = arrived[...].astype(F32)
         products = []
         for l in range(slots):
@@ -194,19 +201,21 @@
             acc = products[0] * (live[0] * hot(coords[0, 0] == r))
             for l in range(1, slots):
                 acc += products[l] * (live[l] * hot(coords[0, l] == r))
-            dst[r * rows : (r + 1) * rows, :] = acc.astype(dst.dtype)
+            put(r, acc)
 
     def rows_of(c):
         return pl.ds(pl.multiple_of(c * chunk, chunk), chunk)
 
-    def to_all(make):
+    def to_all(*makes):
         @pl.loop(0, chips - 1)
         def _(t):
             c = chip_peer(t)
             for k in range(2):
-                make(c, k).start()
-
-        make(chip, 1 - core).start()
+                for make in makes:
+                    make(c, k).start()
+
+        for make in makes:
+            make(chip, 1 - core).start()
 
     def share_all(share, full, s):
         first = core * n_half + chip * chunk
@@ -215,25 +224,31 @@
         place[...] = share[...]
         leaving.append((sized.at[pl.ds(0, total - chunk)], s))
 
-    apply(codes_recv, codes_pick, part)
-    mine = pl.ds(pl.multiple_of(core * n_half, n_half), n_half)
-    theirs = pl.ds(pl.multiple_of((1 - core) * n_half, n_half), n_half)
-    remote(part.at[theirs], pair, 3, mate).start()
-    wait_bytes(pair, recv.at[3])
-    leaving.append((pair, 3))
-    half[...] = part[mine, :] + pair[...]
-
-    @pl.loop(0, chips - 1)
-    def _(t):
-        c = chip_peer(t)
-        remote(half.at[rows_of(c)], gather.at[chip], 4, (p, c * 2 + core)).start()
-
-    gather[chip] = half[rows_of(chip), :]
-    wait_bytes(gather.at[pl.ds(0, chips - 1)], recv.at[4])
-    leaving.append((gather.at[pl.ds(0, chips - 1)], 4))
-    acc = gather[0]
-    for c in range(1, chips):
-        acc += gather[c]
+    def put_part(r, v):
+        n = rows // chunk
+        steps, scale = in_steps(v.reshape(n, chunk, T), 1)
+        part[r * rows : (r + 1) * rows, :] = steps.reshape(rows, T)
+        part_scale[r * n : (r + 1) * n] = scale
+
+    def put_back(r, v):
+        part_b[r * rows : (r + 1) * rows, :] = v.astype(BF16)
+
+    apply(codes_recv, codes_pick, put_part)
+    to_all(
+        lambda c, k: remote(part.at[rows_of(k * chips + c)], gather.at[q], 3, (p, c * 2 + k)),
+        lambda c, k: remote(
+            part_scale.at[k * chips + c], gather_scale.at[q], 4, (p, c * 2 + k)
+        ),
+    )
+    leaving.append((gather.at[pl.ds(0, n_atom - 1)], 3))
+    leaving.append((gather_scale.at[pl.ds(0, n_atom - 1)], 4))
+    gather[q] = part[rows_of(core * chips + chip), :]
+    gather_scale[q] = part_scale[core * chips + chip]
+    wait_bytes(gather.at[pl.ds(0, n_atom - 1)], recv.at[3])
+    wait_bytes(gather_scale.at[pl.ds(0, n_atom - 1)], recv.at[4])
+    acc = jnp.zeros((chunk, T), F32)
+    for c in range(n_atom):
+        acc += gather[c].astype(jnp.int32).astype(F32) * gather_scale[c]
 
     first = (core * chips + chip) * chunk
     snaps = pl.ds(pl.multiple_of(first % rows // 2, V), chunk // 2)
@@ -258,10 +273,7 @@
         turned = swap(plain.astype(F32).reshape(n_dof, V, T)).reshape(rows, T).astype(BF16)
         g = (nn(plain, tiles[l, 0]) - nn(turned, tiles[l, 1])) * live[l]
         corr.append(g.reshape(n_dof, V, T))
-    corr = jnp.concatenate(corr, axis=1)
-    most = jnp.maximum(jnp.max(jnp.abs(corr), axis=1, keepdims=True), 1e-30)
-    corr_send[...] = jnp.round(corr * (STEPS / most)).astype(jnp.int32).astype(jnp.int16)
-    scale_send[...] = most * (1.0 / STEPS)
+    corr_send[...], scale_send[...] = in_steps(jnp.concatenate(corr, axis=1), 1)
 
     @pl.loop(0, n_dof - 1)
     def _(t):
@@ -341,7 +353,7 @@
     thr_dof[p] = thr_part[...]
     wait_bytes(grad_recv.at[pl.ds(0, n_dof - 1)], recv.at[7])
 
-    apply(grad_recv, grad_pick, part_b)
+    apply(grad_recv, grad_pick, put_back)
     to_all(
         lambda c, k: remote(
             part_b.at[rows_of(k * chips + c)], gather_b.at[q], 9, (p, c * 2 + k)
@@ -412,7 +424,6 @@
     rows = V * n_dof
     total = row_tiles * rows
     chunk = total // n_atom
-    chips = n_atom // 2
     z_hi = 4
     hbm = pl.BlockSpec(memory_space=pltpu.HBM)
 
@@ -454,10 +465,10 @@
             pltpu.VMEM((n_dof, slots * V, T), BF16),
             pltpu.VMEM((slots, rows, 2 * T), BF16),
             pltpu.VMEM((slots, rows, 2 * T), BF16),
-            pltpu.VMEM((total, T), F32),
-            pltpu.VMEM((total // 2, T), F32),
-            pltpu.VMEM((total // 2, T), F32),
-            pltpu.VMEM((chips, chunk, T), F32),
+            pltpu.VMEM((total, T), jnp.int16),
+            pltpu.VMEM((n_atom, 1, T), F32),
+            pltpu.VMEM((n_atom, chunk, T), jnp.int16),
+            pltpu.VMEM((n_atom, 1, T), F32),
             pltpu.VMEM((row_tiles, rows, T), BF16),
             pltpu.VMEM((chunk, T), BF16),
             pltpu.VMEM((total, T), BF16),

time: 80.8 us -> 78.7 us (0.974)
  Pallas kernels: 79.3 us -> 77.3 us
    pallas_call x1, Pallas kernels: 77.6 us -> 75.6 us  [local(): pl.pallas_call(functools.partial(kernel, n_dof, n_atom, slots, row_tiles,...]
where the time goes in v4:
time: 78.7 us; the launch traced here: 78.5 us
  Pallas kernels  77.3 us (98%)
  between operations  1.29 us (2%)
    pallas_call x1, Pallas kernels, local(): pl.pallas_call(functools.partial(kernel, n_dof, n_atom, slots, row_tiles,...  75.6 us
    pallas_call x1, Pallas kernels, local(): pl.pallas_call(hand_over, out_shape=tuple((jax.ShapeDtypeStruct(o.shape,...  1.68 us

profile of v4, /device:TPU:1, one launch (start us, length us, event | category | flops | bytes accessed | tf_op | source)
XLA Modules:
  0.0 78.5 jit_solution(12094322540919438852)
XLA Ops:
  1.3 75.6 %shard_map.103 = (bf16[2,4,2048]{2,1,0:T(4,128)(2,1)}, bf16[4,2,128,128]{3,2,1,0:T(8,128)(2,1)}, f32[8]{0:T(128)}) custom-call(bf16[2,64,512]{2,1,0:T(8,128)(2,1)} %received_hbm.1, bf16[2,4,2048]{2,1,0:T(4,128)(2,1)} %codes_hbm.1, bf16[4,2,128,128]{3,2,1,0:T(8,128)(2,1)} %bitcast.5, s32[2,4]{1,0:T(2,128)} %bitcast.6, s32[1,1]{1,0:T(1,128)S(6)} %copy.11.counts_hbm, ...), custom_call_target="tpu_custom_call" | custom-call | tf_op jit(solution)/shard_map/pallas_call | solution.py:430
  76.9 1.7 %shard_map.104 = (bf16[2,4,2048]{2,1,0:T(4,128)(2,1)}, bf16[4,2,128,128]{3,2,1,0:T(8,128)(2,1)}, f32[8]{0:T(128)}) custom-call(bf16[2,4,2048]{2,1,0:T(4,128)(2,1)} %get-tuple-element.9.a, bf16[4,2,128,128]{3,2,1,0:T(8,128)(2,1)} %get-tuple-element.10.b, f32[8]{0:T(128)} %get-tuple-element.11.c), custom_call_target="tpu_custom_call" | custom-call | tf_op jit(solution)/shard_map/pallas_call | solution.py:493

commit v5 on v4

--- a/solution.py
+++ b/solution.py
@@ -361,6 +361,15 @@
     )
     leaving.append((gather_b.at[pl.ds(0, n_atom - 1)], 9))
     gather_b[q] = part_b[rows_of(core * chips + chip), :]
+    wait_bytes(thr_dof.at[pl.ds(0, n_dof - 1)], recv.at[8])
+    row = thr_dof[0]
+    for i in range(1, n_dof):
+        row += thr_dof[i]
+    thr_sum[...] = row
+    to_all(lambda c, k: remote(thr_sum, thr_atom.at[q], 11, (p, c * 2 + k)))
+    leaving.append((thr_atom.at[pl.ds(0, n_atom - 1)], 11))
+    thr_atom[q] = row
+
     for l in range(slots):
         lefts[l] = tn(row_block(resid, l), grad_pick[l])
     wait_bytes(gather_b.at[pl.ds(0, n_atom - 1)], recv.at[9])
@@ -370,14 +379,12 @@
     back_share[...] = acc.astype(BF16)
     share_all(back_share, back, 10)
 
-    wait_bytes(thr_dof.at[pl.ds(0, n_dof - 1)], recv.at[8])
-    row = thr_dof[0]
-    for i in range(1, n_dof):
-        row += thr_dof[i]
-    thr_sum[...] = row
-    to_all(lambda c, k: remote(thr_sum, thr_atom.at[q], 11, (p, c * 2 + k)))
-    leaving.append((thr_atom.at[pl.ds(0, n_atom - 1)], 11))
-    thr_atom[q] = row
+    wait_bytes(thr_atom.at[pl.ds(0, n_atom - 1)], recv.at[11])
+    row = thr_atom[0]
+    for c in range(1, n_atom):
+        row += thr_atom[c]
+    for g in range(groups):
+        thr_out[g] = jnp.sum(jnp.where(lanes == g, row, 0.0))
 
     wait_bytes(sized.at[pl.ds(0, total - chunk)], recv.at[10])
     for l in range(slots):
@@ -387,13 +394,6 @@
         grads_kept[l, 1] = g[:, T:]
         stores.append(pltpu.make_async_copy(grads_kept.at[l], grads_out.at[l], store.at[l]))
         stores[-1].start()
-
-    wait_bytes(thr_atom.at[pl.ds(0, n_atom - 1)], recv.at[11])
-    row = thr_atom[0]
-    for c in range(1, n_atom):
-        row += thr_atom[c]
-    for g in range(groups):
-        thr_out[g] = jnp.sum(jnp.where(lanes == g, row, 0.0))
 
     for copy in stores:
         copy.wait()

time: 78.7 us -> 78.3 us (level)
  no operation moved by 1% of the time
where the time goes in v5:
time: 78.3 us; the launch traced here: 78.1 us
  Pallas kernels  76.8 us (98%)
  between operations  1.29 us (2%)
    pallas_call x1, Pallas kernels, local(): pl.pallas_call(functools.partial(kernel, n_dof, n_atom, slots, row_tiles,...  75.1 us
    pallas_call x1, Pallas kernels, local(): pl.pallas_call(hand_over, out_shape=tuple((jax.ShapeDtypeStruct(o.shape,...  1.68 us

profile of v5, /device:TPU:1, one launch (start us, length us, event | category | flops | bytes accessed | tf_op | source)
XLA Modules:
  0.0 78.1 jit_solution(15894498100009285378)
XLA Ops:
  1.3 75.1 %shard_map.103 = (bf16[2,4,2048]{2,1,0:T(4,128)(2,1)}, bf16[4,2,128,128]{3,2,1,0:T(8,128)(2,1)}, f32[8]{0:T(128)}) custom-call(bf16[2,64,512]{2,1,0:T(8,128)(2,1)} %received_hbm.1, bf16[2,4,2048]{2,1,0:T(4,128)(2,1)} %codes_hbm.1, bf16[4,2,128,128]{3,2,1,0:T(8,128)(2,1)} %bitcast.5, s32[2,4]{1,0:T(2,128)} %bitcast.6, s32[1,1]{1,0:T(1,128)S(6)} %copy.11.counts_hbm, ...), custom_call_target="tpu_custom_call" | custom-call | tf_op jit(solution)/shard_map/pallas_call | solution.py:430
  76.4 1.7 %shard_map.104 = (bf16[2,4,2048]{2,1,0:T(4,128)(2,1)}, bf16[4,2,128,128]{3,2,1,0:T(8,128)(2,1)}, f32[8]{0:T(128)}) custom-call(bf16[2,4,2048]{2,1,0:T(4,128)(2,1)} %get-tuple-element.9.a, bf16[4,2,128,128]{3,2,1,0:T(8,128)(2,1)} %get-tuple-element.10.b, f32[8]{0:T(128)} %get-tuple-element.11.c), custom_call_target="tpu_custom_call" | custom-call | tf_op jit(solution)/shard_map/pallas_call | solution.py:493
